TPU v7x, 32 devices: a whole 2x2x4 slice. The times are simulated.
32 devices in a mesh: groups: 2 (over y), space: 4 (over z), member: 2 (over x), chan: 2 (over core).
Axes of the slice: x: 2, y: 2, z: 4, core: 2. Of those that a mesh axis runs over, the one named last changes fastest.
Arguments:
- mesh_state: bfloat16 [4, 96, 128, 256], P(('groups', 'member'), ('space', 'chan')), parts along dimension 0, may hold values from -6 to 6
- boundary: bfloat16 [4, 32, 128, 256], P(('groups', 'member'), 'space'), parts along dimension 0, may hold values from -6 to 6
- boundary_send: int32 [8, 4, 3], P('groups'), parts along dimension 0, may hold values from 0 to 7
- boundary_count: int32 [8, 4], P('groups'), parts along dimension 0, may hold values from 0 to 3, as said below
- grid_edges: int32 [192, 4], P(('groups', 'space', 'chan')), parts along dimension 0, may hold values from 0 to 11
- edge_tiles: int32 [16], P(('groups', 'space')), parts along dimension 0, may hold values from 0 to 23
- halo_source: int32 [64], P(('groups', 'space')), parts along dimension 0, may hold values from 0 to 7
- halo_count: int32 [8], P(('groups', 'space')), parts along dimension 0, may hold values from 1 to 8, as said below
- mesh_edges: int32 [192, 8], P(('groups', 'space', 'chan')), parts along dimension 0, may hold values from 0 to 31
- edge_first: bfloat16 [2, 2, 256, 256], replicated, may hold values from -0.25 to 0.25
- edge_bias: float32 [2, 256], replicated, may hold values from -3 to 3
- edge_second: bfloat16 [2, 256, 256], replicated, may hold values from -0.125 to 0.125
- node_first: bfloat16 [2, 2, 256, 256], replicated, may hold values from -0.25 to 0.25
- node_bias: float32 [2, 256], replicated, may hold values from -3 to 3
- node_second: bfloat16 [2, 256, 256], replicated, may hold values from -0.375 to 0.375
- node_gain: float32 [2, 256], replicated, may hold values from 0.1 to 1.9
Outputs:
- processed: bfloat16 [4, 96, 128, 256], P(('groups', 'member'), ('space', 'chan')), parts along dimension 0
There are 2 independent parts, one for each index of `groups`. A program takes and returns all parts, laid end to end along the dimension named above; an argument that names none is the same for every part. Nothing has to cross between parts.
Inputs may be any that keep to these rules, and one draw needn't show every extreme that they name: `boundary_count`: 3 is reached by some pair. `halo_count`: 8 is reached by some partition.
All inputs are finite; a program needn't handle non-finite values.
Results may differ from a plain program's by a relative error of at most 0.0063.
Values may be sent and summed in bfloat16 or wider, within the bound.
A program may use at most 64 MiB of HBM per device.

v0:
```python
import jax
import jax.numpy as jnp
from jax import lax
from jax.sharding import PartitionSpec as P


def layer_norm(values, gain):
    center = values - jnp.mean(values, axis=-1, keepdims=True)
    spread = jnp.mean(center * center, axis=-1, keepdims=True)
    return center * lax.rsqrt(spread + 1e-05) * gain


def project(tiles, weight):
    return jnp.einsum("mtrh,hk->mtrk", tiles, weight, preferred_element_type=jnp.float32)


def select_table(index, count, dtype):
    return (index[:, None] == jnp.arange(count, dtype=jnp.int32)[None, :]).astype(dtype)


def select_tiles(table, tiles):
    return jnp.einsum("sj,mjrh->msrh", table, tiles, preferred_element_type=jnp.float32).astype(
        tiles.dtype
    )


def chooser(wanted, live_slot, shards):
    span = shards.shape[1]
    hits = (wanted[:, None] == jnp.arange(span, dtype=jnp.int32)[None, :]) & live_slot[:, None]
    return jnp.einsum(
        "sj,mjrh->msrh", hits.astype(shards.dtype), shards, preferred_element_type=jnp.float32
    )


def interact(targets, sources, edge_index, layer_id, weights):
    edge_first, edge_bias, edge_second, node_first, node_bias, node_second, node_gain = weights
    source_proj = project(sources, edge_first[layer_id, 0])
    target_proj = project(targets, edge_first[layer_id, 1]) + edge_bias[layer_id]
    source_count = source_proj.shape[1]
    running = jnp.zeros(target_proj.shape, jnp.float32)
    for column in range(edge_index.shape[1]):
        table = select_table(edge_index[:, column], source_count, jnp.float32)
        picked = jnp.einsum("tj,mjrh->mtrh", table, source_proj, precision=lax.Precision.HIGHEST)
        running = running + jax.nn.silu(picked + target_proj)
    hidden = running.astype(jnp.bfloat16)
    aggregate = project(hidden, edge_second[layer_id]).astype(jnp.bfloat16)
    inner_hidden = jax.nn.silu(
        project(targets, node_first[layer_id, 0])
        + project(aggregate, node_first[layer_id, 1])
        + node_bias[layer_id]
    ).astype(jnp.bfloat16)
    node_sum = project(inner_hidden, node_second[layer_id])
    return (targets.astype(jnp.float32) + layer_norm(node_sum, node_gain[layer_id])).astype(
        jnp.bfloat16
    )


def body(
    mesh_state,
    boundary,
    boundary_send,
    boundary_count,
    grid_edges,
    edge_tiles,
    halo_source,
    halo_count,
    mesh_edges,
    edge_first,
    edge_bias,
    edge_second,
    node_first,
    node_bias,
    node_second,
    node_gain,
):
    weights = (edge_first, edge_bias, edge_second, node_first, node_bias, node_second, node_gain)
    own_index = lax.axis_index("space")
    local_tiles = boundary.shape[1]
    capacity = boundary_send.shape[2]
    slot_range = jnp.arange(capacity, dtype=jnp.int32)
    tile_rows = jnp.take(boundary_send, own_index, axis=0)
    live_slot = slot_range[None, :] < jnp.take(boundary_count, own_index, axis=0)[:, None]
    table = select_table(tile_rows.reshape(-1), local_tiles, boundary.dtype)
    table = table * live_slot.reshape(-1)[:, None].astype(boundary.dtype)
    picked = select_tiles(table, boundary)
    slot_tiles = lax.all_to_all(picked, "space", split_axis=1, concat_axis=1, tiled=True)
    encoded = interact(mesh_state, slot_tiles, grid_edges, 0, weights)
    partition_encoded = lax.all_gather(encoded, "chan", axis=1, tiled=True)
    edge_table = select_table(edge_tiles, partition_encoded.shape[1], partition_encoded.dtype)
    edge_states = select_tiles(edge_table, partition_encoded)
    halo_slots = halo_source.shape[0]
    halo_live = jnp.arange(halo_slots, dtype=jnp.int32) < halo_count[0]
    halo_tiles = chooser(
        halo_source, halo_live, lax.all_gather(edge_states, "space", axis=1, tiled=True)
    ).astype(jnp.bfloat16)
    sources = jnp.concatenate([partition_encoded, halo_tiles], axis=1)
    return interact(encoded, sources, mesh_edges, 1, weights)


def solution(mesh):
    in_specs = (
        P(("groups", "member"), ("space", "chan"), None, None),
        P(("groups", "member"), "space", None, None),
        P("groups", None, None),
        P("groups", None),
        P(("groups", "space", "chan"), None),
        P(("groups", "space")),
        P(("groups", "space")),
        P(("groups", "space")),
        P(("groups", "space", "chan"), None),
        P(),
        P(),
        P(),
        P(),
        P(),
        P(),
        P(),
    )
    out_specs = P(("groups", "member"), ("space", "chan"), None, None)
    return jax.shard_map(body, mesh=mesh, in_specs=in_specs, out_specs=out_specs, check_vma=False)
```

profile of v0, /device:TPU:0, one launch (start us, length us, event | category | flops | bytes accessed | tf_op | source)
XLA Modules:
  0.0 116.3 jit_solution(8027784417538262760)
XLA Ops:
  10.0 6.3 %all-to-all-start = ((bf16[1,12,128,256]{3,2,0,1:T(8,128)(2,1)}), bf16[1,12,128,256]{3,2,0,1:T(8,128)(2,1)S(1)}, u32[]{:S(2)}, u32[]{:S(2)}) async-start(bf16[1,12,128,256]{3,2,0,1:T(8,128)(2,1)} %copy.57), calls=%async_computation | async-start | bytes 1572864 | tf_op jit(solution)/shard_map/all_to_all | solution.py:86
  16.5 1.5 %fusion.37 = f32[12,128,256]{2,1,0:T(8,128)} fusion(bf16[1,12,128,256]{3,2,1,0:T(8,128)(2,1)S(1)} %copy-done.2, bf16[2,2,256,256]{3,2,1,0:T(8,128)(2,1)S(1)} %copy-done.5), kind=kOutput, calls=%fused_computation.56 | convolution fusion | flops 201326592 | bytes 2490368 | tf_op jit(solution)/shard_map/mtrh,hk->mtrk/dot_general | solution.py:14
  18.0 2.4 %fusion.39 = f32[12,128,256]{2,1,0:T(8,128)} fusion(bf16[1,12,128,256]{3,2,1,0:T(8,128)(2,1)S(1)} %copy-done.2, bf16[2,2,256,256]{3,2,1,0:T(8,128)(2,1)} %param.28), kind=kOutput, calls=%fused_computation.58 | convolution fusion | flops 201326592 | bytes 2490368 | tf_op jit(solution)/shard_map/mtrh,hk->mtrk/dot_general | solution.py:14
  20.4 16.0 %all-to-all-done = bf16[1,12,128,256]{3,2,0,1:T(8,128)(2,1)S(1)} async-done(((bf16[1,12,128,256]{3,2,0,1:T(8,128)(2,1)}), bf16[1,12,128,256]{3,2,0,1:T(8,128)(2,1)S(1)}, u32[]{:S(2)}, u32[]{:S(2)}) %all-to-all-start) | async-done | bytes 786464 | tf_op jit(solution)/shard_map/all_to_all | solution.py:86
  36.8 2.3 %fusion = f32[128,256,12]{1,2,0:T(8,128)S(1)} fusion(f32[12,128,256]{2,1,0:T(8,128)S(1)} %fusion.35, s32[12]{0:T(128)S(1)} %get-tuple-element.43), kind=kOutput, calls=%fused_computation | convolution fusion | flops 56623248 | bytes 3145776 | tf_op jit(solution)/shard_map/tj,mjrh->mtrh/dot_general | solution.py:43
  39.1 2.3 %fusion.2 = f32[128,256,12]{1,2,0:T(8,128)S(1)} fusion(f32[12,128,256]{2,1,0:T(8,128)S(1)} %fusion.35, s32[12]{0:T(128)S(1)} %get-tuple-element.44), kind=kOutput, calls=%fused_computation.2 | convolution fusion | flops 56623248 | bytes 3145776 | tf_op jit(solution)/shard_map/tj,mjrh->mtrh/dot_general | solution.py:43
  41.4 2.3 %fusion.4 = f32[128,256,12]{1,2,0:T(8,128)S(1)} fusion(f32[12,128,256]{2,1,0:T(8,128)S(1)} %fusion.35, s32[12]{0:T(128)S(1)} %get-tuple-element.42), kind=kOutput, calls=%fused_computation.4 | convolution fusion | flops 56623248 | bytes 3145776 | tf_op jit(solution)/shard_map/tj,mjrh->mtrh/dot_general | solution.py:43
  43.8 5.0 %fusion.20 = bf16[12,128,256]{2,0,1:T(8,128)(2,1)S(1)} fusion(f32[128,256,12]{1,2,0:T(8,128)S(1)} %fusion, f32[128,256,12]{1,2,0:T(8,128)S(1)} %fusion.2, f32[128,256,12]{1,2,0:T(8,128)S(1)} %fusion.4, f32[12,128,256]{2,1,0:T(8,128)S(1)} %copy-done.3, f32[12,128,256]{2,1,0:T(8,128)S(1)} %fusion.35, f32[256]{0:T(256)S(1)} %bitcast.355, ...), kind=kOutput, calls=%fused_computation.44 | convolution fusion | flops 66453648 | bytes 8651824 | tf_op jit(solution)/shard_map/tj,mjrh->mtrh/dot_general | solution.py:43
  50.3 2.5 %fusion.144 = (f32[12,128]{1,0:T(8,128)S(1)}, f32[12,128,256]{2,1,0:T(8,128)S(1)}) fusion(bf16[2,256,256]{2,1,0:T(8,128)(2,1)} %param.30, f32[12,128,256]{2,1,0:T(8,128)} %fusion.39, bf16[12,128,256]{2,1,0:T(8,128)(2,1)} %convolution_convert_fusion.2, f32[256]{0:T(256)S(1)} %bitcast.354, bf16[2,2,256,256]{3,2,1,0:T(8,128)(2,1)} %param.28), kind=kOutput, calls=%fused_computation.179 | convolution fusion | flops 405797376 | bytes 4201472 | tf_op jit(solution)/shard_map/mtrh,hk->mtrk/dot_general | solution.py:14
  55.5 1.5 %fusion.31 = f32[12,128,256]{2,1,0:T(8,128)S(1)} fusion(bf16[1,12,128,256]{3,2,1,0:T(8,128)(2,1)} %fusion.15, bf16[2,2,256,256]{3,2,1,0:T(8,128)(2,1)S(1)} %copy-done.5), kind=kOutput, calls=%fused_computation.50 | convolution fusion | flops 201326592 | bytes 2490368 | tf_op jit(solution)/shard_map/mtrh,hk->mtrk/dot_general | solution.py:14
  57.0 2.4 %fusion.33 = f32[12,128,256]{2,1,0:T(8,128)} fusion(bf16[1,12,128,256]{3,2,1,0:T(8,128)(2,1)S(1)} %copy-done.1, bf16[2,2,256,256]{3,2,1,0:T(8,128)(2,1)} %param.28), kind=kOutput, calls=%fused_computation.52 | convolution fusion | flops 201326592 | bytes 2490368 | tf_op jit(solution)/shard_map/mtrh,hk->mtrk/dot_general | solution.py:14
  59.5 4.4 %all-gather.2.cloned.1.call-done = bf16[1,24,128,256]{3,2,0,1:T(8,128)(2,1)} async-done(((bf16[1,12,128,256]{3,2,0,1:T(8,128)(2,1)}), bf16[1,24,128,256]{3,2,0,1:T(8,128)(2,1)}) %all-gather.2.cloned.1.call-update) | async-done | bytes 1572880 | tf_op jit(solution)/shard_map/all_gather | solution.py:88
  63.8 2.5 %fusion.28 = bf16[1,2,128,256]{3,1,2,0:T(2,128)(2,1)S(1)} fusion(bf16[1,24,128,256]{3,2,0,1:T(8,128)(2,1)} %all-gather.2.cloned.1.call-done, s32[2]{0:T(128)S(1)} %copy-done.15), kind=kOutput, calls=%fused_computation.49 | convolution fusion | flops 3211312 | bytes 1703944 | tf_op jit(solution)/shard_map/sj,mjrh->msrh/dot_general | solution.py:22
  66.4 16.5 %all_gather.7 = bf16[1,8,128,256]{3,2,0,1:T(8,128)(2,1)S(1)} all-gather(bf16[1,2,128,256]{3,2,0,1:T(8,128)(2,1)S(1)} %copy.66), channel_id=1, replica_groups=mesh['groups'=2,'space'=4,'member'=2,'chan'=2] {'space'}, dimensions={1}, use_global_device_ids=true | all-gather | bytes 655360 | tf_op jit(solution)/shard_map/all_gather | solution.py:94
  83.6 1.5 %fusion.8 = f32[32,128,256]{2,0,1:T(8,128)S(1)} fusion(bf16[32,128,256]{2,1,0:T(8,128)(2,1)S(1)} %maximum_bitcast_fusion, bf16[2,2,256,256]{3,2,1,0:T(8,128)(2,1)S(1)} %copy-done.5), kind=kOutput, calls=%fused_computation.21 | convolution fusion | flops 536870912 | bytes 6422528 | tf_op jit(solution)/shard_map/mtrh,hk->mtrk/dot_general | solution.py:14
  85.2 1.6 %fusion.102 = f32[128,256,12]{1,2,0:T(8,128)S(1)} fusion(f32[32,128,256]{2,0,1:T(8,128)S(1)} %fusion.8, s32[12]{0:T(128)S(1)} %get-tuple-element.28), kind=kOutput, calls=%fused_computation.122 | convolution fusion | flops 150995328 | bytes 5767216 | tf_op jit(solution)/shard_map/tj,mjrh->mtrh/dot_general | solution.py:43
  86.8 1.6 %fusion.105 = f32[128,256,12]{1,2,0:T(8,128)S(1)} fusion(f32[32,128,256]{2,0,1:T(8,128)S(1)} %fusion.8, s32[12]{0:T(128)S(1)} %get-tuple-element.34), kind=kOutput, calls=%fused_computation.124 | convolution fusion | flops 150995328 | bytes 5767216 | tf_op jit(solution)/shard_map/tj,mjrh->mtrh/dot_general | solution.py:43
  88.4 1.6 %fusion.87 = f32[128,256,12]{1,2,0:T(8,128)S(1)} fusion(f32[32,128,256]{2,0,1:T(8,128)S(1)} %fusion.8, s32[12]{0:T(128)S(1)} %get-tuple-element.33), kind=kOutput, calls=%fused_computation.112 | convolution fusion | flops 150995328 | bytes 5767216 | tf_op jit(solution)/shard_map/tj,mjrh->mtrh/dot_general | solution.py:43
  90.1 1.6 %fusion.90 = f32[128,256,12]{1,2,0:T(8,128)S(1)} fusion(f32[32,128,256]{2,0,1:T(8,128)S(1)} %fusion.8, s32[12]{0:T(128)S(1)} %get-tuple-element.32), kind=kOutput, calls=%fused_computation.114 | convolution fusion | flops 150995328 | bytes 5767216 | tf_op jit(solution)/shard_map/tj,mjrh->mtrh/dot_general | solution.py:43
  91.7 1.6 %fusion.93 = f32[128,256,12]{1,2,0:T(8,128)S(1)} fusion(f32[32,128,256]{2,0,1:T(8,128)S(1)} %fusion.8, s32[12]{0:T(128)S(1)} %get-tuple-element.31), kind=kOutput, calls=%fused_computation.116 | convolution fusion | flops 150995328 | bytes 5767216 | tf_op jit(solution)/shard_map/tj,mjrh->mtrh/dot_general | solution.py:43
  93.4 1.6 %fusion.96 = f32[128,256,12]{1,2,0:T(8,128)S(1)} fusion(f32[32,128,256]{2,0,1:T(8,128)S(1)} %fusion.8, s32[12]{0:T(128)S(1)} %get-tuple-element.30), kind=kOutput, calls=%fused_computation.118 | convolution fusion | flops 150995328 | bytes 5767216 | tf_op jit(solution)/shard_map/tj,mjrh->mtrh/dot_general | solution.py:43
  95.0 1.9 %fusion.99 = f32[128,256,12]{1,2,0:T(8,128)S(1)} fusion(f32[32,128,256]{2,0,1:T(8,128)S(1)} %fusion.8, s32[12]{0:T(128)S(1)} %get-tuple-element.29), kind=kOutput, calls=%fused_computation.120 | convolution fusion | flops 150995328 | bytes 5767216 | tf_op jit(solution)/shard_map/tj,mjrh->mtrh/dot_general | solution.py:43
  97.0 6.6 %fusion.19 = bf16[12,128,256]{2,0,1:T(8,128)(2,1)S(1)} fusion(f32[32,128,256]{2,0,1:T(8,128)S(1)} %fusion.8, f32[128,256,12]{1,2,0:T(8,128)S(1)} %fusion.105, f32[128,256,12]{1,2,0:T(8,128)S(1)} %fusion.102, f32[128,256,12]{1,2,0:T(8,128)S(1)} %fusion.99, f32[128,256,12]{1,2,0:T(8,128)S(1)} %fusion.96, f32[128,256,12]{1,2,0:T(8,128)S(1)} %fusion.93, ...), kind=kOutput, calls=%fused_computation.43 | convolution fusion | flops 170262912 | bytes 17564720 | tf_op jit(solution)/shard_map/tj,mjrh->mtrh/dot_general | solution.py:43
  105.0 2.5 %fusion.147 = (f32[12,128]{1,0:T(8,128)S(1)}, f32[12,128,256]{2,1,0:T(8,128)S(1)}) fusion(bf16[2,256,256]{2,1,0:T(8,128)(2,1)S(1)} %copy-done.14, f32[12,128,256]{2,1,0:T(8,128)} %fusion.33, bf16[12,128,256]{2,1,0:T(8,128)(2,1)} %convolution_convert_fusion.1, f32[256]{0:T(256)S(1)} %bitcast.352, bf16[2,2,256,256]{3,2,1,0:T(8,128)(2,1)} %param.28), kind=kOutput, calls=%fused_computation.180 | convolution fusion | flops 405797376 | bytes 4201472 | tf_op jit(solution)/shard_map/mtrh,hk->mtrk/dot_general | solution.py:14
  (63 shorter events, 11.4 us)
Async XLA Ops:
  6.5 1.8 %copy-start = (bf16[1,8,128,256]{3,2,1,0:T(8,128)(2,1)S(1)}, bf16[1,8,128,256]{3,2,1,0:T(8,128)(2,1)}, u32[]{:S(2)}) copy-start(bf16[1,8,128,256]{3,2,1,0:T(8,128)(2,1)} %param.17) | copy-start | bytes 1572868
  8.8 7.5 %copy-start.9 = (s32[12,4]{0,1:T(4,128)S(1)}, s32[12,4]{0,1:T(4,128)}, u32[]{:S(2)}) copy-start(s32[12,4]{0,1:T(4,128)} %param.20) | copy-start | bytes 580
  8.9 7.5 %copy-start.10 = (f32[2,256]{1,0:T(2,128)S(1)}, f32[2,256]{1,0:T(2,128)}, u32[]{:S(2)}) copy-start(f32[2,256]{1,0:T(2,128)} %param.26) | copy-start | bytes 6148
  8.9 7.5 %copy-start.11 = (f32[2,256]{1,0:T(2,128)S(1)}, f32[2,256]{1,0:T(2,128)}, u32[]{:S(2)}) copy-start(f32[2,256]{1,0:T(2,128)} %param.29) | copy-start | bytes 6148
  8.9 7.5 %copy-start.12 = (f32[2,256]{1,0:T(2,128)S(1)}, f32[2,256]{1,0:T(2,128)}, u32[]{:S(2)}) copy-start(f32[2,256]{1,0:T(2,128)} %param.31) | copy-start | bytes 6148
  8.9 7.5 %copy-start.2 = (bf16[1,12,128,256]{3,2,1,0:T(8,128)(2,1)S(1)}, bf16[1,12,128,256]{3,2,1,0:T(8,128)(2,1)}, u32[]{:S(2)}) copy-start(bf16[1,12,128,256]{3,2,1,0:T(8,128)(2,1)} %param.16) | copy-start | bytes 2359300
  8.9 7.5 %copy-start.5 = (bf16[2,2,256,256]{3,2,1,0:T(8,128)(2,1)S(1)}, bf16[2,2,256,256]{3,2,1,0:T(8,128)(2,1)}, u32[]{:S(2)}) copy-start(bf16[2,2,256,256]{3,2,1,0:T(8,128)(2,1)} %param.25) | copy-start | bytes 1572868
  10.0 26.4 %all-to-all-start = ((bf16[1,12,128,256]{3,2,0,1:T(8,128)(2,1)}), bf16[1,12,128,256]{3,2,0,1:T(8,128)(2,1)S(1)}, u32[]{:S(2)}, u32[]{:S(2)}) async-start(bf16[1,12,128,256]{3,2,0,1:T(8,128)(2,1)} %copy.57), calls=%async_computation | async-start | bytes 1572864 | tf_op jit(solution)/shard_map/all_to_all | solution.py:86
  16.4 47.5 %all-gather.2.cloned.1.call-start = ((), (), s32[]{:S(2)}) async-start(), calls=%async_computation.1 | async-start | bytes 2359296 | tf_op jit(solution)/shard_map/all_gather | solution.py:88
  41.4 2.3 %copy-start.3 = (f32[12,128,256]{2,1,0:T(8,128)S(1)}, f32[12,128,256]{2,1,0:T(8,128)}, u32[]{:S(2)}) copy-start(f32[12,128,256]{2,1,0:T(8,128)} %fusion.37) | copy-start | bytes 4718596
  43.8 5.1 %copy-start.6 = (bf16[2,256,256]{2,1,0:T(8,128)(2,1)S(1)}, bf16[2,256,256]{2,1,0:T(8,128)(2,1)}, u32[]{:S(2)}) copy-start(bf16[2,256,256]{2,1,0:T(8,128)(2,1)} %param.27) | copy-start | bytes 786436
  53.3 2.2 %copy-start.8 = (s32[12,8]{0,1:T(8,128)S(1)}, s32[12,8]{0,1:T(8,128)}, u32[]{:S(2)}) copy-start(s32[12,8]{0,1:T(8,128)} %param.24) | copy-start | bytes 1156
  54.7 2.3 %copy-start.1 = (bf16[1,12,128,256]{3,2,1,0:T(8,128)(2,1)S(1)}, bf16[1,12,128,256]{3,2,1,0:T(8,128)(2,1)}, u32[]{:S(2)}) copy-start(bf16[1,12,128,256]{3,2,1,0:T(8,128)(2,1)} %fusion.15) | copy-start | bytes 2359300
  55.5 8.3 %copy-start.15 = (s32[2]{0:T(128)S(1)}, s32[2]{0:T(128)}, u32[]{:S(2)}) copy-start(s32[2]{0:T(128)} %param.21) | copy-start | bytes 28
  57.0 25.9 %copy-start.13 = (s32[8]{0:T(128)S(1)}, s32[8]{0:T(128)}, u32[]{:S(2)}) copy-start(s32[8]{0:T(128)} %param.22) | copy-start | bytes 100
  63.8 19.6 %copy-start.4 = (bf16[1,24,128,256]{3,2,0,1:T(8,128)(2,1)S(1)}, bf16[1,24,128,256]{3,2,0,1:T(8,128)(2,1)}, u32[]{:S(2)}) copy-start(bf16[1,24,128,256]{3,2,0,1:T(8,128)(2,1)} %all-gather.2.cloned.1.call-done) | copy-start | bytes 4718596
  96.9 6.6 %copy-start.7 = (bf16[2,256,256]{2,1,0:T(8,128)(2,1)S(1)}, bf16[2,256,256]{2,1,0:T(8,128)(2,1)}, u32[]{:S(2)}) copy-start(bf16[2,256,256]{2,1,0:T(8,128)(2,1)} %param.27) | copy-start | bytes 786436
  97.0 8.1 %copy-start.14 = (bf16[2,256,256]{2,1,0:T(8,128)(2,1)S(1)}, bf16[2,256,256]{2,1,0:T(8,128)(2,1)}, u32[]{:S(2)}) copy-start(bf16[2,256,256]{2,1,0:T(8,128)(2,1)} %param.30) | copy-start | bytes 786436
Sparse Core Ops, SparseCore 0:
  54.9 8.9 all-gather.1
where the time goes:
time: 117 us; the launch traced here: 116 us
  matrix products  51.4 us (44%)
  waiting for transfers between devices  20.4 us (17%)
  blocking collectives  16.5 us (14%)
  between operations  14.5 us (12%)
  starting transfers between devices  6.32 us (5%)
  other arithmetic  5.5 us (5%)
  local copies, waits for them, and re-layouts  1.63 us (1%)
    dot_general x12, matrix products, interact(): jnp.einsum('tj,mjrh->mtrh', table, source_proj, precision=lax.Precision.H...  30.2 us
    dot_general x10, matrix products, project(): jnp.einsum('mtrh,hk->mtrk', tiles, weight, preferred_element_type=jnp.flo...  17.7 us
    all_gather x1, blocking collectives, body(): lax.all_gather(edge_states, 'space', axis=1, tiled=True)  16.5 us
    all_to_all x1, waiting for transfers between devices, body(): lax.all_to_all(picked, 'space', split_axis=1, concat_axis=1, tiled=True)  16 us
    all_to_all x1, starting transfers between devices, body(): lax.all_to_all(picked, 'space', split_axis=1, concat_axis=1, tiled=True)  6.31 us
    all_gather x1, waiting for transfers between devices, body(): partition_encoded = lax.all_gather(encoded, 'chan', axis=1, tiled=True)  4.37 us
    dot_general x2, matrix products, select_tiles(): jnp.einsum('sj,mjrh->msrh', table, tiles, preferred_element_type=jnp.floa...  3.01 us
    convert_element_type x2, other arithmetic, interact(): (targets.astype(jnp.float32) + layer_norm(node_sum, node_gain[layer_id]))...  2.75 us
  transfers between devices with their start and end apart: 2, of which 2 were waited for; matrix products, arithmetic and copies ran while one was open for 7% of the time, Pallas kernels for 0%

commit v1 on v0

v1 whole, which is shorter than its diff:
```python
import functools

import jax
import jax.numpy as jnp
from jax import lax
from jax.experimental import pallas as pl
from jax.experimental.pallas import tpu as pltpu
from jax.sharding import PartitionSpec as P

MESH = pl.DeviceIdType.MESH
ROWS = 16
UNROLL = 4


def dot(left, right):
    return jnp.dot(left, right, preferred_element_type=jnp.float32)


def kernel(
    n,
    mesh_state,
    boundary,
    grid_edges,
    mesh_edges,
    boundary_send,
    boundary_count,
    edge_tiles,
    halo_source,
    halo_count,
    edge_first,
    edge_second,
    node_first,
    node_second,
    edge_bias,
    node_bias,
    node_gain,
    out,
    bound,
    picked,
    slots,
    targets,
    encoded,
    edge_out,
    edge_in,
    result,
    first,
    second,
    node_a,
    node_b,
    source_proj,
    target_proj,
    hidden,
    own_grid,
    own_mesh,
    far_grid,
    far_mesh,
    grid_index,
    mesh_index,
    halo_table,
    local_sem,
    state_sem,
    state_send,
    state_recv,
    index_send,
    index_recv,
    slot_send,
    slot_recv,
    halo_send,
    halo_recv,
    out_local,
    out_send,
    out_recv,
):
    space, chan = lax.axis_index("space"), lax.axis_index("chan")
    other = 1 - chan
    half = bound.shape[1]
    chunks = half // ROWS
    tiles_own = mesh_state.shape[1]
    tiles = 2 * tiles_own
    cap = boundary_send.shape[2]
    edges = edge_tiles.shape[0]
    halo = halo_source.shape[0]
    zero_tile = source_proj.shape[0] - 1
    features = targets.shape[2]

    def start_row(side, chunk):
        return pl.multiple_of(side * half + chunk * ROWS, ROWS)

    get_bound = pltpu.make_async_copy(
        boundary.at[0, :, pl.ds(start_row(chan, 0), half), :], bound, local_sem.at[0]
    )
    get_bound.start()
    index_copies = [
        pltpu.make_async_copy(grid_edges, own_grid, local_sem.at[1]),
        pltpu.make_async_copy(mesh_edges, own_mesh, local_sem.at[2]),
    ]
    weight_copies = [
        pltpu.make_async_copy(edge_first, first, local_sem.at[3]),
        pltpu.make_async_copy(edge_second, second, local_sem.at[4]),
        pltpu.make_async_copy(node_first, node_a, local_sem.at[5]),
        pltpu.make_async_copy(node_second, node_b, local_sem.at[6]),
    ]
    state_local = pltpu.make_async_copy(
        mesh_state.at[0, :, pl.ds(start_row(chan, 0), half), :],
        targets.at[pl.ds(chan * tiles_own, tiles_own)],
        state_sem,
    )
    state_local.start()
    for copy in index_copies + weight_copies:
        copy.start()

    barrier = pltpu.get_barrier_semaphore()
    for step in range(1, n):
        pl.semaphore_signal(
            barrier, inc=1, device_id={"space": lax.rem(space + step, n)}, device_id_type=MESH
        )
    pl.semaphore_signal(barrier, inc=1, device_id={"chan": other}, device_id_type=MESH)

    get_bound.wait()

    def pick(partition, chunk):
        values = []
        for c in range(cap):
            tile = bound[boundary_send[space, partition, c], pl.ds(chunk * ROWS, ROWS), :]
            live = jnp.where(c < boundary_count[space, partition], 1.0, 0.0)
            values.append((tile.astype(jnp.float32) * live).astype(jnp.bfloat16))
        return values

    for chunk in range(chunks):
        for step in range(1, n):
            for c, value in enumerate(pick(lax.rem(space + step, n), chunk)):
                picked[chunk, step - 1, c] = value

    pl.semaphore_wait(barrier, n)

    sends = []
    slot_copies = []
    for chunk in range(chunks):
        row = []
        for step in range(1, n):
            copy = pltpu.make_async_remote_copy(
                src_ref=picked.at[chunk, step - 1],
                dst_ref=slots.at[chunk, space],
                send_sem=slot_send.at[chunk, step - 1],
                recv_sem=slot_recv.at[chunk, step - 1],
                device_id={"space": lax.rem(space + step, n)},
                device_id_type=MESH,
            )
            copy.start()
            row.append(copy)
        slot_copies.append(row)
        sends += row

    far_index = []
    for number, (source, target) in enumerate(((grid_edges, far_grid), (mesh_edges, far_mesh))):
        copy = pltpu.make_async_remote_copy(
            src_ref=source,
            dst_ref=target,
            send_sem=index_send.at[number],
            recv_sem=index_recv.at[number],
            device_id={"chan": other},
            device_id_type=MESH,
        )
        copy.start()
        far_index.append(copy)
    sends += far_index
    state_copies = []
    for chunk in range(chunks):
        copy = pltpu.make_async_remote_copy(
            src_ref=mesh_state.at[0, :, pl.ds(start_row(other, chunk), ROWS), :],
            dst_ref=targets.at[pl.ds(chan * tiles_own, tiles_own), pl.ds(chunk * ROWS, ROWS), :],
            send_sem=state_send.at[chunk],
            recv_sem=state_recv.at[chunk],
            device_id={"chan": other},
            device_id_type=MESH,
        )
        copy.start()
        state_copies.append(copy)
    sends += state_copies

    for chunk in range(chunks):
        for c, value in enumerate(pick(space, chunk)):
            slots[chunk, space, c] = value
    for tile in range(tiles):
        halo_table[tile] = tile
    for h in range(halo):
        halo_table[tiles + h] = jnp.where(
            h < halo_count[0], tiles + halo_source[h], zero_tile
        )
    source_proj[zero_tile] = jnp.zeros((ROWS, features), jnp.float32)
    for copy in index_copies:
        copy.wait()
    for copy in far_index:
        copy.wait_recv()

    def index_step(tile, carry):
        near, far = chan * tiles_own + tile, other * tiles_own + tile
        for k in range(grid_index.shape[1]):
            grid_index[near, k] = own_grid[tile, k]
            grid_index[far, k] = far_grid[tile, k]
        for k in range(mesh_index.shape[1]):
            mesh_index[near, k] = halo_table[own_mesh[tile, k]]
            mesh_index[far, k] = halo_table[far_mesh[tile, k]]
        return carry

    lax.fori_loop(0, tiles_own, index_step, 0)
    for copy in weight_copies:
        copy.wait()
    state_local.wait()

    def interact(layer, target, index):
        target_proj[...] = (
            (dot(target, first[layer, 1]) + edge_bias[layer : layer + 1, :]) * 0.5
        ).reshape(target_proj.shape)

        def tile_step(tile, carry):
            base = target_proj[tile]
            total = None
            for k in range(index.shape[1]):
                value = source_proj[index[tile, k]] + base
                term = value * jnp.tanh(value) + value
                total = term if total is None else total + term
            hidden[tile] = total.astype(jnp.bfloat16)
            return carry

        lax.fori_loop(0, tiles, tile_step, 0, unroll=UNROLL)
        sums = hidden[...].reshape(tiles * ROWS, features)
        aggregate = dot(sums, second[layer]).astype(jnp.bfloat16)
        value = 0.5 * (
            dot(target, node_a[layer, 0])
            + dot(aggregate, node_a[layer, 1])
            + node_bias[layer : layer + 1, :]
        )
        inner = (value * jnp.tanh(value) + value).astype(jnp.bfloat16)
        node_sum = dot(inner, node_b[layer])
        center = node_sum - jnp.mean(node_sum, axis=-1, keepdims=True)
        spread = jnp.mean(center * center, axis=-1, keepdims=True)
        normed = center * lax.rsqrt(spread + 1e-05) * node_gain[layer : layer + 1, :]
        return (target.astype(jnp.float32) + normed).astype(jnp.bfloat16)

    def project(tiles_in, layer, begin):
        count = tiles_in.shape[0] // ROWS
        source_proj[begin : begin + count] = (dot(tiles_in, first[layer, 0]) * 0.5).reshape(
            count, ROWS, features
        )

    halo_copies = []

    def encode(chunk):
        rows = pl.ds(chunk * ROWS, ROWS)
        state_copies[chunk].wait_recv()
        for copy in slot_copies[chunk]:
            copy.wait_recv()
        project(slots[chunk].reshape(n * cap * ROWS, features), 0, 0)
        target = targets[:, rows, :].reshape(tiles * ROWS, features)
        encoded[:, rows, :] = interact(0, target, grid_index).reshape(tiles, ROWS, features)
        for j in range(edges):
            value = encoded[edge_tiles[j], rows, :]
            edge_out[chunk, j] = value
            edge_in[chunk, space, j] = value
        row = []
        for step in range(1, n):
            copy = pltpu.make_async_remote_copy(
                src_ref=edge_out.at[chunk],
                dst_ref=edge_in.at[chunk, space],
                send_sem=halo_send.at[chunk, step - 1],
                recv_sem=halo_recv.at[chunk, step - 1],
                device_id={"space": lax.rem(space + step, n)},
                device_id_type=MESH,
            )
            copy.start()
            row.append(copy)
        halo_copies.append(row)

    local_outs, far_outs = [], []

    def process(chunk):
        rows = pl.ds(chunk * ROWS, ROWS)
        target = encoded[:, rows, :].reshape(tiles * ROWS, features)
        project(target, 1, 0)
        for copy in halo_copies[chunk]:
            copy.wait_recv()
        project(edge_in[chunk].reshape(n * edges * ROWS, features), 1, tiles)
        result[:, rows, :] = interact(1, target, mesh_index).reshape(tiles, ROWS, features)
        place = out.at[0, :, pl.ds(start_row(chan, chunk), ROWS), :]
        far = pltpu.make_async_remote_copy(
            src_ref=result.at[pl.ds(other * tiles_own, tiles_own), rows, :],
            dst_ref=place,
            send_sem=out_send.at[chunk],
            recv_sem=out_recv.at[chunk],
            device_id={"chan": other},
            device_id_type=MESH,
        )
        far.start()
        far_outs.append(far)
        near = pltpu.make_async_copy(
            result.at[pl.ds(chan * tiles_own, tiles_own), rows, :], place, out_local.at[chunk]
        )
        near.start()
        local_outs.append(near)

    for chunk in range(chunks):
        encode(chunk)
    for chunk in range(chunks):
        process(chunk)

    for copy in sends:
        copy.wait_send()
    for row in halo_copies:
        for copy in row:
            copy.wait_send()
    for copy in local_outs + far_outs:
        copy.wait()


def body(
    n,
    mesh_state,
    boundary,
    boundary_send,
    boundary_count,
    grid_edges,
    edge_tiles,
    halo_source,
    halo_count,
    mesh_edges,
    edge_first,
    edge_bias,
    edge_second,
    node_first,
    node_bias,
    node_second,
    node_gain,
):
    _, own, tile, features = mesh_state.shape
    half = tile // 2
    chunks = half // ROWS
    tiles = 2 * own
    cap = boundary_send.shape[2]
    edges = edge_tiles.shape[0]
    halo = halo_source.shape[0]
    count = max(n * cap, tiles + n * edges) + 1
    bf16, f32, i32 = jnp.bfloat16, jnp.float32, jnp.int32
    dma = pltpu.SemaphoreType.DMA
    scratch = [
        pltpu.VMEM((boundary.shape[1], half, features), bf16),
        pltpu.VMEM((chunks, n - 1, cap, ROWS, features), bf16),
        pltpu.VMEM((chunks, n, cap, ROWS, features), bf16),
        pltpu.VMEM((tiles, half, features), bf16),
        pltpu.VMEM((tiles, half, features), bf16),
        pltpu.VMEM((chunks, edges, ROWS, features), bf16),
        pltpu.VMEM((chunks, n, edges, ROWS, features), bf16),
        pltpu.VMEM((tiles, half, features), bf16),
        pltpu.VMEM(edge_first.shape, bf16),
        pltpu.VMEM(edge_second.shape, bf16),
        pltpu.VMEM(node_first.shape, bf16),
        pltpu.VMEM(node_second.shape, bf16),
        pltpu.VMEM((count, ROWS, features), f32),
        pltpu.VMEM((tiles, ROWS, features), f32),
        pltpu.VMEM((tiles, ROWS, features), bf16),
        pltpu.SMEM(grid_edges.shape, i32),
        pltpu.SMEM(mesh_edges.shape, i32),
        pltpu.SMEM(grid_edges.shape, i32),
        pltpu.SMEM(mesh_edges.shape, i32),
        pltpu.SMEM((tiles, grid_edges.shape[1]), i32),
        pltpu.SMEM((tiles, mesh_edges.shape[1]), i32),
        pltpu.SMEM((tiles + halo,), i32),
        dma((7,)),
        dma,
        dma((chunks,)),
        dma((chunks,)),
        dma((2,)),
        dma((2,)),
        dma((chunks, n - 1)),
        dma((chunks, n - 1)),
        dma((chunks, n - 1)),
        dma((chunks, n - 1)),
        dma((chunks,)),
        dma((chunks,)),
        dma((chunks,)),
    ]
    hbm = pl.BlockSpec(memory_space=pl.ANY)
    smem = pl.BlockSpec(memory_space=pltpu.SMEM)
    vmem = pl.BlockSpec(memory_space=pltpu.VMEM)
    return pl.pallas_call(
        functools.partial(kernel, n),
        out_shape=jax.ShapeDtypeStruct(mesh_state.shape, bf16),
        in_specs=[hbm] * 4 + [smem] * 5 + [hbm] * 4 + [vmem] * 3,
        out_specs=hbm,
        scratch_shapes=scratch,
        compiler_params=pltpu.CompilerParams(
            collective_id=0, has_side_effects=True, vmem_limit_bytes=40 * 1024 * 1024
        ),
    )(
        mesh_state,
        boundary,
        grid_edges,
        mesh_edges,
        boundary_send,
        boundary_count,
        edge_tiles,
        halo_source,
        halo_count,
        edge_first,
        edge_second,
        node_first,
        node_second,
        edge_bias,
        node_bias,
        node_gain,
    )


def solution(mesh):
    in_specs = (
        P(("groups", "member"), ("space", "chan"), None, None),
        P(("groups", "member"), "space", None, None),
        P("groups", None, None),
        P("groups", None),
        P(("groups", "space", "chan"), None),
        P(("groups", "space")),
        P(("groups", "space")),
        P(("groups", "space")),
        P(("groups", "space", "chan"), None),
        P(),
        P(),
        P(),
        P(),
        P(),
        P(),
        P(),
    )
    out_specs = P(("groups", "member"), ("space", "chan"), None, None)
    return jax.shard_map(
        functools.partial(body, mesh.shape["space"]),
        mesh=mesh,
        in_specs=in_specs,
        out_specs=out_specs,
        check_vma=False,
    )
```

time: 117 us -> 37.7 us (0.32)
  matrix products: 51.4 us -> 0 us
  Pallas kernels: 0 us -> 27.3 us
  waiting for transfers between devices: 20.4 us -> 0 us
  blocking collectives: 16.5 us -> 0 us
  between operations: 14.5 us -> 0.7 us
  local copies, waits for them, and re-layouts: 1.63 us -> 9.24 us
  starting transfers between devices: 6.32 us -> 0 us
  other arithmetic: 5.5 us -> 0 us
    dot_general x25 -> x0, matrix products: 51.4 us -> none  [the longest x12 30.2 us: interact(): jnp.einsum('tj,mjrh->mtrh', table, source_proj, precision=lax.Precision.H...]
    pallas_call x0 -> x1, Pallas kernels: none -> 27.3 us  [body(): pl.pallas_call(functools.partial(kernel, n), out_shape=jax.ShapeDtypeStru...]
    all_gather x1 -> x0, blocking collectives: 16.5 us -> none  [body(): lax.all_gather(edge_states, 'space', axis=1, tiled=True)]
    all_to_all x1 -> x0, waiting for transfers between devices: 16 us -> none  [body(): lax.all_to_all(picked, 'space', split_axis=1, concat_axis=1, tiled=True)]
    unnamed x32, local copies, waits for them, and re-layouts: 0.09 us -> 9.24 us
    all_to_all x1 -> x0, starting transfers between devices: 6.31 us -> none  [body(): lax.all_to_all(picked, 'space', split_axis=1, concat_axis=1, tiled=True)]
    all_gather x1 -> x0, waiting for transfers between devices: 4.37 us -> none  [body(): partition_encoded = lax.all_gather(encoded, 'chan', axis=1, tiled=True)]
    convert_element_type x3 -> x0, other arithmetic: 2.83 us -> none  [the longest x2 2.75 us: interact(): (targets.astype(jnp.float32) + layer_norm(node_sum, node_gain[layer_id]))...]
  transfers between devices with their start and end apart: 2 -> 0, of which waited for: 2 -> 0; matrix products, arithmetic and copies ran while one was open for 7% -> 0% of each run, Pallas kernels for 0% -> 0%
where the time goes in v1:
time: 37.7 us; the launch traced here: 37.2 us
  Pallas kernels  27.3 us (72%)
  local copies, waits for them, and re-layouts  9.24 us (25%)
  between operations  0.7 us (2%)
    pallas_call x1, Pallas kernels, body(): pl.pallas_call(functools.partial(kernel, n), out_shape=jax.ShapeDtypeStru...  27.3 us
    unnamed x32, local copies, waits for them, and re-layouts  9.24 us

profile of v1, /device:TPU:0, one launch (start us, length us, event | category | flops | bytes accessed | tf_op | source)
XLA Modules:
  0.0 37.2 jit_solution(12609508114627631473)
XLA Ops:
  0.7 0.0 copy-start.13
  0.7 0.8 %copy.19.boundary_send = s32[4,4,3]{2,1,0:T(4,128)S(1)} copy(s32[4,4,3]{1,0,2:T(4,128)} %param.18) | data formatting | bytes 384 | tf_op args[2]
  1.5 0.0 copy-done.13
  1.5 0.0 copy-start.12
  1.5 0.1 copy.17.grid_edges
  1.6 0.6 %copy-done.12 = s32[12,8]{0,1:T(8,128)S(1)} copy-done((s32[12,8]{0,1:T(8,128)S(1)}, s32[12,8]{0,1:T(8,128)}, u32[]{:S(2)}) %copy-start.12) | copy-done | bytes 408
  2.2 0.0 copy-start.6
  2.2 0.0 copy-start.10
  2.2 0.0 copy-start.11
  2.2 0.1 copy.18.mesh_edges
  2.3 0.6 %copy-done.6 = s32[4,4]{1,0:T(4,128)S(1)} copy-done((s32[4,4]{1,0:T(4,128)S(1)}, s32[4,4]{1,0:T(4,128)}, u32[]{:S(2)}) %copy-start.6) | copy-done | bytes 88
  2.8 0.0 copy-done.7
  2.9 0.0 copy-done.8
  2.9 0.0 copy-done.9
  2.9 0.0 copy-done.10
  2.9 0.0 copy-done.11
  2.9 1.1 %copy-done = bf16[1,12,128,256]{3,2,1,0:T(8,128)(2,1)S(1)} copy-done((bf16[1,12,128,256]{3,2,1,0:T(8,128)(2,1)S(1)}, bf16[1,12,128,256]{3,2,1,0:T(8,128)(2,1)}, u32[]{:S(2)}) %copy-start) | copy-done | bytes 786456
  4.0 1.0 %copy-done.1 = bf16[1,8,128,256]{3,2,1,0:T(8,128)(2,1)S(1)} copy-done((bf16[1,8,128,256]{3,2,1,0:T(8,128)(2,1)S(1)}, bf16[1,8,128,256]{3,2,1,0:T(8,128)(2,1)}, u32[]{:S(2)}) %copy-start.1) | copy-done | bytes 524312
  5.1 1.0 %copy-done.2 = bf16[2,2,256,256]{3,2,1,0:T(8,128)(2,1)S(1)} copy-done((bf16[2,2,256,256]{3,2,1,0:T(8,128)(2,1)S(1)}, bf16[2,2,256,256]{3,2,1,0:T(8,128)(2,1)}, u32[]{:S(2)}) %copy-start.2) | copy-done | bytes 524312
  6.1 1.0 %copy-done.3 = bf16[2,2,256,256]{3,2,1,0:T(8,128)(2,1)S(1)} copy-done((bf16[2,2,256,256]{3,2,1,0:T(8,128)(2,1)S(1)}, bf16[2,2,256,256]{3,2,1,0:T(8,128)(2,1)}, u32[]{:S(2)}) %copy-start.3) | copy-done | bytes 524312
  7.2 0.9 %copy-done.4 = bf16[2,256,256]{2,1,0:T(8,128)(2,1)S(1)} copy-done((bf16[2,256,256]{2,1,0:T(8,128)(2,1)S(1)}, bf16[2,256,256]{2,1,0:T(8,128)(2,1)}, u32[]{:S(2)}) %copy-start.4) | copy-done | bytes 262168
  8.1 0.9 %copy-done.5 = bf16[2,256,256]{2,1,0:T(8,128)(2,1)S(1)} copy-done((bf16[2,256,256]{2,1,0:T(8,128)(2,1)S(1)}, bf16[2,256,256]{2,1,0:T(8,128)(2,1)}, u32[]{:S(2)}) %copy-start.5) | copy-done | bytes 262168
  9.1 27.3 %shard_map.154 = bf16[1,12,128,256]{3,2,1,0:T(8,128)(2,1)S(1)} custom-call(bf16[1,12,128,256]{3,2,1,0:T(8,128)(2,1)S(1)} %copy-done, bf16[1,8,128,256]{3,2,1,0:T(8,128)(2,1)S(1)} %copy-done.1, s32[12,4]{1,0:T(8,128)S(1)} %copy.17.grid_edges, s32[12,8]{1,0:T(8,128)S(1)} %copy.18.mesh_edges, s32[4,4,3]{2,1,0:T(4,128)S(1)} %copy.19.boundary_send, ...), custom_call_target="tpu_custom_call" | custom-call | tf_op jit(solution)/shard_map/pallas_call | solution.py:385
  36.3 0.9 %copy.22 = bf16[1,12,128,256]{3,2,1,0:T(8,128)(2,1)} copy(bf16[1,12,128,256]{3,2,1,0:T(8,128)(2,1)S(1)} %shard_map.154) | data formatting | bytes 1572864
  (9 shorter events, 0.0 us)
Async XLA Ops:
  0.7 0.8 %copy-start.13 = (s32[12,4]{0,1:T(4,128)S(1)}, s32[12,4]{0,1:T(4,128)}, u32[]{:S(2)}) copy-start(s32[12,4]{0,1:T(4,128)} %param.20) | copy-start | bytes 580
  1.5 0.7 %copy-start.12 = (s32[12,8]{0,1:T(8,128)S(1)}, s32[12,8]{0,1:T(8,128)}, u32[]{:S(2)}) copy-start(s32[12,8]{0,1:T(8,128)} %param.24) | copy-start | bytes 1156
  2.2 0.7 %copy-start.6 = (s32[4,4]{1,0:T(4,128)S(1)}, s32[4,4]{1,0:T(4,128)}, u32[]{:S(2)}) copy-start(s32[4,4]{1,0:T(4,128)} %boundary_count.1) | copy-start | bytes 196
  2.2 0.7 %copy-start.7 = (f32[2,256]{1,0:T(2,128)S(1)}, f32[2,256]{1,0:T(2,128)}, u32[]{:S(2)}) copy-start(f32[2,256]{1,0:T(2,128)} %edge_bias.1) | copy-start | bytes 6148
  2.2 0.7 %copy-start.8 = (f32[2,256]{1,0:T(2,128)S(1)}, f32[2,256]{1,0:T(2,128)}, u32[]{:S(2)}) copy-start(f32[2,256]{1,0:T(2,128)} %node_bias.1) | copy-start | bytes 6148
  2.2 0.7 %copy-start.9 = (f32[2,256]{1,0:T(2,128)S(1)}, f32[2,256]{1,0:T(2,128)}, u32[]{:S(2)}) copy-start(f32[2,256]{1,0:T(2,128)} %node_gain.1) | copy-start | bytes 6148
  2.2 0.7 %copy-start.10 = (s32[2]{0:T(128)S(1)}, s32[2]{0:T(128)}, u32[]{:S(2)}) copy-start(s32[2]{0:T(128)} %edge_tiles.1) | copy-start | bytes 28
  2.2 0.7 %copy-start.11 = (s32[8]{0:T(128)S(1)}, s32[8]{0:T(128)}, u32[]{:S(2)}) copy-start(s32[8]{0:T(128)} %halo_source.1) | copy-start | bytes 100
  2.9 1.1 %copy-start = (bf16[1,12,128,256]{3,2,1,0:T(8,128)(2,1)S(1)}, bf16[1,12,128,256]{3,2,1,0:T(8,128)(2,1)}, u32[]{:S(2)}) copy-start(bf16[1,12,128,256]{3,2,1,0:T(8,128)(2,1)} %mesh_state.1) | copy-start | bytes 2359300
  4.0 1.0 %copy-start.1 = (bf16[1,8,128,256]{3,2,1,0:T(8,128)(2,1)S(1)}, bf16[1,8,128,256]{3,2,1,0:T(8,128)(2,1)}, u32[]{:S(2)}) copy-start(bf16[1,8,128,256]{3,2,1,0:T(8,128)(2,1)} %boundary.1) | copy-start | bytes 1572868
  5.1 1.0 %copy-start.2 = (bf16[2,2,256,256]{3,2,1,0:T(8,128)(2,1)S(1)}, bf16[2,2,256,256]{3,2,1,0:T(8,128)(2,1)}, u32[]{:S(2)}) copy-start(bf16[2,2,256,256]{3,2,1,0:T(8,128)(2,1)} %edge_first.1) | copy-start | bytes 1572868
  6.1 1.0 %copy-start.3 = (bf16[2,2,256,256]{3,2,1,0:T(8,128)(2,1)S(1)}, bf16[2,2,256,256]{3,2,1,0:T(8,128)(2,1)}, u32[]{:S(2)}) copy-start(bf16[2,2,256,256]{3,2,1,0:T(8,128)(2,1)} %node_first.1) | copy-start | bytes 1572868
  7.2 0.9 %copy-start.4 = (bf16[2,256,256]{2,1,0:T(8,128)(2,1)S(1)}, bf16[2,256,256]{2,1,0:T(8,128)(2,1)}, u32[]{:S(2)}) copy-start(bf16[2,256,256]{2,1,0:T(8,128)(2,1)} %edge_second.1) | copy-start | bytes 786436
  8.1 0.9 %copy-start.5 = (bf16[2,256,256]{2,1,0:T(8,128)(2,1)S(1)}, bf16[2,256,256]{2,1,0:T(8,128)(2,1)}, u32[]{:S(2)}) copy-start(bf16[2,256,256]{2,1,0:T(8,128)(2,1)} %node_second.1) | copy-start | bytes 786436

commit v2 on v1

--- a/solution.py
+++ b/solution.py
@@ -8,8 +8,9 @@
 from jax.sharding import PartitionSpec as P
 
 MESH = pl.DeviceIdType.MESH
-ROWS = 16
+ROWS = 32
 UNROLL = 4
+SEND_ORDER = (2, 0, 1)
 
 
 def dot(left, right):
@@ -22,19 +23,27 @@
     boundary,
     grid_edges,
     mesh_edges,
+    boundary_send_in,
+    boundary_count_in,
+    edge_tiles_in,
+    halo_source_in,
+    halo_count_in,
+    edge_first,
+    edge_second,
+    node_first,
+    node_second,
+    edge_bias_in,
+    node_bias_in,
+    node_gain_in,
+    out,
     boundary_send,
     boundary_count,
     edge_tiles,
     halo_source,
     halo_count,
-    edge_first,
-    edge_second,
-    node_first,
-    node_second,
     edge_bias,
     node_bias,
     node_gain,
-    out,
     bound,
     picked,
     slots,
@@ -77,7 +86,7 @@
     chunks = half // ROWS
     tiles_own = mesh_state.shape[1]
     tiles = 2 * tiles_own
-    cap = boundary_send.shape[2]
+    cap = boundary_send.shape[0]
     edges = edge_tiles.shape[0]
     halo = halo_source.shape[0]
     zero_tile = source_proj.shape[0] - 1
@@ -90,11 +99,23 @@
         boundary.at[0, :, pl.ds(start_row(chan, 0), half), :], bound, local_sem.at[0]
     )
     get_bound.start()
+    table_copies = [
+        pltpu.make_async_copy(boundary_send_in, boundary_send, local_sem.at[7]),
+        pltpu.make_async_copy(boundary_count_in, boundary_count, local_sem.at[8]),
+    ]
+    for copy in table_copies:
+        copy.start()
     index_copies = [
+        pltpu.make_async_copy(edge_tiles_in, edge_tiles, local_sem.at[9]),
+        pltpu.make_async_copy(halo_source_in, halo_source, local_sem.at[10]),
+        pltpu.make_async_copy(halo_count_in, halo_count, local_sem.at[11]),
         pltpu.make_async_copy(grid_edges, own_grid, local_sem.at[1]),
         pltpu.make_async_copy(mesh_edges, own_mesh, local_sem.at[2]),
     ]
     weight_copies = [
+        pltpu.make_async_copy(edge_bias_in, edge_bias, local_sem.at[12]),
+        pltpu.make_async_copy(node_bias_in, node_bias, local_sem.at[13]),
+        pltpu.make_async_copy(node_gain_in, node_gain, local_sem.at[14]),
         pltpu.make_async_copy(edge_first, first, local_sem.at[3]),
         pltpu.make_async_copy(edge_second, second, local_sem.at[4]),
         pltpu.make_async_copy(node_first, node_a, local_sem.at[5]),
@@ -117,11 +138,13 @@
     pl.semaphore_signal(barrier, inc=1, device_id={"chan": other}, device_id_type=MESH)
 
     get_bound.wait()
+    for copy in table_copies:
+        copy.wait()
 
     def pick(partition, chunk):
         values = []
         for c in range(cap):
-            tile = bound[boundary_send[space, partition, c], pl.ds(chunk * ROWS, ROWS), :]
+            tile = bound[boundary_send[c, space, partition], pl.ds(chunk * ROWS, ROWS), :]
             live = jnp.where(c < boundary_count[space, partition], 1.0, 0.0)
             values.append((tile.astype(jnp.float32) * live).astype(jnp.bfloat16))
         return values
@@ -181,6 +204,8 @@
     for chunk in range(chunks):
         for c, value in enumerate(pick(space, chunk)):
             slots[chunk, space, c] = value
+    for copy in index_copies:
+        copy.wait()
     for tile in range(tiles):
         halo_table[tile] = tile
     for h in range(halo):
@@ -188,19 +213,17 @@
             h < halo_count[0], tiles + halo_source[h], zero_tile
         )
     source_proj[zero_tile] = jnp.zeros((ROWS, features), jnp.float32)
-    for copy in index_copies:
-        copy.wait()
     for copy in far_index:
         copy.wait_recv()
 
     def index_step(tile, carry):
         near, far = chan * tiles_own + tile, other * tiles_own + tile
         for k in range(grid_index.shape[1]):
-            grid_index[near, k] = own_grid[tile, k]
-            grid_index[far, k] = far_grid[tile, k]
+            grid_index[near, k] = own_grid[k, tile]
+            grid_index[far, k] = far_grid[k, tile]
         for k in range(mesh_index.shape[1]):
-            mesh_index[near, k] = halo_table[own_mesh[tile, k]]
-            mesh_index[far, k] = halo_table[far_mesh[tile, k]]
+            mesh_index[near, k] = halo_table[own_mesh[k, tile]]
+            mesh_index[far, k] = halo_table[far_mesh[k, tile]]
         return carry
 
     lax.fori_loop(0, tiles_own, index_step, 0)
@@ -343,6 +366,14 @@
     bf16, f32, i32 = jnp.bfloat16, jnp.float32, jnp.int32
     dma = pltpu.SemaphoreType.DMA
     scratch = [
+        pltpu.SMEM(tuple(boundary_send.shape[axis] for axis in SEND_ORDER), i32),
+        pltpu.SMEM(boundary_count.shape, i32),
+        pltpu.SMEM(edge_tiles.shape, i32),
+        pltpu.SMEM(halo_source.shape, i32),
+        pltpu.SMEM(halo_count.shape, i32),
+        pltpu.VMEM(edge_bias.shape, f32),
+        pltpu.VMEM(node_bias.shape, f32),
+        pltpu.VMEM(node_gain.shape, f32),
         pltpu.VMEM((boundary.shape[1], half, features), bf16),
         pltpu.VMEM((chunks, n - 1, cap, ROWS, features), bf16),
         pltpu.VMEM((chunks, n, cap, ROWS, features), bf16),
@@ -358,14 +389,14 @@
         pltpu.VMEM((count, ROWS, features), f32),
         pltpu.VMEM((tiles, ROWS, features), f32),
         pltpu.VMEM((tiles, ROWS, features), bf16),
-        pltpu.SMEM(grid_edges.shape, i32),
-        pltpu.SMEM(mesh_edges.shape, i32),
-        pltpu.SMEM(grid_edges.shape, i32),
-        pltpu.SMEM(mesh_edges.shape, i32),
+        pltpu.SMEM(grid_edges.shape[::-1], i32),
+        pltpu.SMEM(mesh_edges.shape[::-1], i32),
+        pltpu.SMEM(grid_edges.shape[::-1], i32),
+        pltpu.SMEM(mesh_edges.shape[::-1], i32),
         pltpu.SMEM((tiles, grid_edges.shape[1]), i32),
         pltpu.SMEM((tiles, mesh_edges.shape[1]), i32),
         pltpu.SMEM((tiles + halo,), i32),
-        dma((7,)),
+        dma((15,)),
         dma,
         dma((chunks,)),
         dma((chunks,)),
@@ -379,24 +410,22 @@
         dma((chunks,)),
         dma((chunks,)),
     ]
-    hbm = pl.BlockSpec(memory_space=pl.ANY)
-    smem = pl.BlockSpec(memory_space=pltpu.SMEM)
-    vmem = pl.BlockSpec(memory_space=pltpu.VMEM)
+    hbm = pl.BlockSpec(memory_space=pltpu.HBM)
     return pl.pallas_call(
         functools.partial(kernel, n),
         out_shape=jax.ShapeDtypeStruct(mesh_state.shape, bf16),
-        in_specs=[hbm] * 4 + [smem] * 5 + [hbm] * 4 + [vmem] * 3,
+        in_specs=[hbm] * 16,
         out_specs=hbm,
         scratch_shapes=scratch,
         compiler_params=pltpu.CompilerParams(
-            collective_id=0, has_side_effects=True, vmem_limit_bytes=40 * 1024 * 1024
+            collective_id=0, has_side_effects=True, vmem_limit_bytes=60 * 1024 * 1024
         ),
     )(
         mesh_state,
         boundary,
-        grid_edges,
-        mesh_edges,
-        boundary_send,
+        grid_edges.T,
+        mesh_edges.T,
+        jnp.transpose(boundary_send, SEND_ORDER),
         boundary_count,
         edge_tiles,
         halo_source,

time: 37.7 us -> 29.3 us (0.78)
  local copies, waits for them, and re-layouts: 9.24 us -> 2.06 us
  Pallas kernels: 27.3 us -> 26.4 us
    unnamed x32 -> x1, local copies, waits for them, and re-layouts: 9.24 us -> 2.06 us
    pallas_call x1, Pallas kernels: 27.3 us -> 26.4 us  [body(): pl.pallas_call(functools.partial(kernel, n), out_shape=jax.ShapeDtypeStru...]
where the time goes in v2:
time: 29.3 us; the launch traced here: 29.1 us
  Pallas kernels  26.4 us (90%)
  local copies, waits for them, and re-layouts  2.06 us (7%)
  between operations  0.66 us (2%)
    pallas_call x1, Pallas kernels, body(): pl.pallas_call(functools.partial(kernel, n), out_shape=jax.ShapeDtypeStru...  26.4 us
    unnamed x1, local copies, waits for them, and re-layouts  2.06 us

profile of v2, /device:TPU:0, one launch (start us, length us, event | category | flops | bytes accessed | tf_op | source)
XLA Modules:
  0.0 29.1 jit_solution(16223851944474459807)
XLA Ops:
  0.7 26.4 %shard_map.154 = bf16[1,12,128,256]{3,2,1,0:T(8,128)(2,1)} custom-call(bf16[1,12,128,256]{3,2,1,0:T(8,128)(2,1)} %mesh_state.1, bf16[1,8,128,256]{3,2,1,0:T(8,128)(2,1)} %boundary.1, s32[4,12]{1,0:T(4,128)} %bitcast.5, s32[8,12]{1,0:T(8,128)} %bitcast.4, s32[3,4,4]{2,1,0:T(4,128)} %bitcast.3, s32[4,4]{1,0:T(4,128)} %boundary_count_in.1, s32[2]{0:T(128)} %edge_tiles_in.1, ...), custom_call_target="tpu_custom_call" | custom-call | tf_op jit(solution)/shard_map/pallas_call | solution.py:414
  27.0 2.1 %copy.19 = bf16[1,12,128,256]{3,2,1,0:T(8,128)(2,1)} copy(bf16[1,12,128,256]{3,2,1,0:T(8,128)(2,1)} %shard_map.154) | data formatting | bytes 1572864

commit v3 on v2

--- a/solution.py
+++ b/solution.py
@@ -95,6 +95,13 @@
     def start_row(side, chunk):
         return pl.multiple_of(side * half + chunk * ROWS, ROWS)
 
+    barrier = pltpu.get_barrier_semaphore()
+    for step in range(1, n):
+        pl.semaphore_signal(
+            barrier, inc=1, device_id={"space": lax.rem(space + step, n)}, device_id_type=MESH
+        )
+    pl.semaphore_signal(barrier, inc=1, device_id={"chan": other}, device_id_type=MESH)
+
     get_bound = pltpu.make_async_copy(
         boundary.at[0, :, pl.ds(start_row(chan, 0), half), :], bound, local_sem.at[0]
     )
@@ -130,13 +137,6 @@
     for copy in index_copies + weight_copies:
         copy.start()
 
-    barrier = pltpu.get_barrier_semaphore()
-    for step in range(1, n):
-        pl.semaphore_signal(
-            barrier, inc=1, device_id={"space": lax.rem(space + step, n)}, device_id_type=MESH
-        )
-    pl.semaphore_signal(barrier, inc=1, device_id={"chan": other}, device_id_type=MESH)
-
     get_bound.wait()
     for copy in table_copies:
         copy.wait()
@@ -149,16 +149,14 @@
             values.append((tile.astype(jnp.float32) * live).astype(jnp.bfloat16))
         return values
 
+    sends = []
+    slot_copies = []
     for chunk in range(chunks):
         for step in range(1, n):
             for c, value in enumerate(pick(lax.rem(space + step, n), chunk)):
                 picked[chunk, step - 1, c] = value
-
-    pl.semaphore_wait(barrier, n)
-
-    sends = []
-    slot_copies = []
-    for chunk in range(chunks):
+        if chunk == 0:
+            pl.semaphore_wait(barrier, n)
         row = []
         for step in range(1, n):
             copy = pltpu.make_async_remote_copy(
@@ -413,9 +411,9 @@
     hbm = pl.BlockSpec(memory_space=pltpu.HBM)
     return pl.pallas_call(
         functools.partial(kernel, n),
-        out_shape=jax.ShapeDtypeStruct(mesh_state.shape, bf16),
+        out_shape=pltpu.VMEM(mesh_state.shape, bf16),
         in_specs=[hbm] * 16,
-        out_specs=hbm,
+        out_specs=pl.BlockSpec(memory_space=pltpu.VMEM),
         scratch_shapes=scratch,
         compiler_params=pltpu.CompilerParams(
             collective_id=0, has_side_effects=True, vmem_limit_bytes=60 * 1024 * 1024

time: 29.3 us -> 27.9 us (0.952)
  local copies, waits for them, and re-layouts: 2.06 us -> 0.88 us
    unnamed x1, local copies, waits for them, and re-layouts: 2.06 us -> 0.88 us
where the time goes in v3:
time: 27.9 us; the launch traced here: 27.8 us
  Pallas kernels  26.2 us (94%)
  local copies, waits for them, and re-layouts  0.88 us (3%)
  between operations  0.66 us (2%)
    pallas_call x1, Pallas kernels, body(): pl.pallas_call(functools.partial(kernel, n), out_shape=pltpu.VMEM(mesh_st...  26.2 us
    unnamed x1, local copies, waits for them, and re-layouts  0.88 us

profile of v3, /device:TPU:0, one launch (start us, length us, event | category | flops | bytes accessed | tf_op | source)
XLA Modules:
  0.0 27.8 jit_solution(10109260703228749586)
XLA Ops:
  0.7 26.2 %shard_map.154 = bf16[1,12,128,256]{3,2,1,0:T(8,128)(2,1)S(1)} custom-call(bf16[1,12,128,256]{3,2,1,0:T(8,128)(2,1)} %mesh_state.1, bf16[1,8,128,256]{3,2,1,0:T(8,128)(2,1)} %boundary.1, s32[4,12]{1,0:T(4,128)} %bitcast.5, s32[8,12]{1,0:T(8,128)} %bitcast.4, s32[3,4,4]{2,1,0:T(4,128)} %bitcast.3, s32[4,4]{1,0:T(4,128)} %boundary_count_in.1, s32[2]{0:T(128)} %edge_tiles_in.1, ...), custom_call_target="tpu_custom_call" | custom-call | tf_op jit(solution)/shard_map/pallas_call | solution.py:412
  26.9 0.9 %copy.18 = bf16[1,12,128,256]{3,2,1,0:T(8,128)(2,1)} copy(bf16[1,12,128,256]{3,2,1,0:T(8,128)(2,1)S(1)} %shard_map.154) | data formatting | bytes 1572864

commit v4 on v3

--- a/solution.py
+++ b/solution.py
@@ -229,10 +229,12 @@
         copy.wait()
     state_local.wait()
 
-    def interact(layer, target, index):
+    def project_target(layer, target):
         target_proj[...] = (
             (dot(target, first[layer, 1]) + edge_bias[layer : layer + 1, :]) * 0.5
         ).reshape(target_proj.shape)
+
+    def interact(layer, target, index):
 
         def tile_step(tile, carry):
             base = target_proj[tile]
@@ -270,10 +272,11 @@
     def encode(chunk):
         rows = pl.ds(chunk * ROWS, ROWS)
         state_copies[chunk].wait_recv()
+        target = targets[:, rows, :].reshape(tiles * ROWS, features)
+        project_target(0, target)
         for copy in slot_copies[chunk]:
             copy.wait_recv()
         project(slots[chunk].reshape(n * cap * ROWS, features), 0, 0)
-        target = targets[:, rows, :].reshape(tiles * ROWS, features)
         encoded[:, rows, :] = interact(0, target, grid_index).reshape(tiles, ROWS, features)
         for j in range(edges):
             value = encoded[edge_tiles[j], rows, :]
@@ -299,6 +302,7 @@
         rows = pl.ds(chunk * ROWS, ROWS)
         target = encoded[:, rows, :].reshape(tiles * ROWS, features)
         project(target, 1, 0)
+        project_target(1, target)
         for copy in halo_copies[chunk]:
             copy.wait_recv()
         project(edge_in[chunk].reshape(n * edges * ROWS, features), 1, tiles)

time: 27.9 us -> 27.6 us (0.989)
  Pallas kernels: 26.2 us -> 25.9 us
    pallas_call x1, Pallas kernels: 26.2 us -> 25.9 us  [body(): pl.pallas_call(functools.partial(kernel, n), out_shape=pltpu.VMEM(mesh_st...]
where the time goes in v4:
time: 27.6 us; the launch traced here: 27.4 us
  Pallas kernels  25.9 us (94%)
  local copies, waits for them, and re-layouts  0.88 us (3%)
  between operations  0.66 us (2%)
    pallas_call x1, Pallas kernels, body(): pl.pallas_call(functools.partial(kernel, n), out_shape=pltpu.VMEM(mesh_st...  25.9 us
    unnamed x1, local copies, waits for them, and re-layouts  0.88 us

profile of v4, /device:TPU:0, one launch (start us, length us, event | category | flops | bytes accessed | tf_op | source)
XLA Modules:
  0.0 27.4 jit_solution(16844774678063205564)
XLA Ops:
  0.7 25.9 %shard_map.154 = bf16[1,12,128,256]{3,2,1,0:T(8,128)(2,1)S(1)} custom-call(bf16[1,12,128,256]{3,2,1,0:T(8,128)(2,1)} %mesh_state.1, bf16[1,8,128,256]{3,2,1,0:T(8,128)(2,1)} %boundary.1, s32[4,12]{1,0:T(4,128)} %bitcast.5, s32[8,12]{1,0:T(8,128)} %bitcast.4, s32[3,4,4]{2,1,0:T(4,128)} %bitcast.3, s32[4,4]{1,0:T(4,128)} %boundary_count_in.1, s32[2]{0:T(128)} %edge_tiles_in.1, ...), custom_call_target="tpu_custom_call" | custom-call | tf_op jit(solution)/shard_map/pallas_call | solution.py:416
  26.5 0.9 %copy.18 = bf16[1,12,128,256]{3,2,1,0:T(8,128)(2,1)} copy(bf16[1,12,128,256]{3,2,1,0:T(8,128)(2,1)S(1)} %shard_map.154) | data formatting | bytes 1572864
